TPU v7x, 32 devices: a whole 2x2x4 slice. The times are simulated.
32 devices in a mesh: wide: 8 (over y, x, core), loop: 4 (over z).
Axes of the slice: x: 2, y: 2, z: 4, core: 2. Of those that a mesh axis runs over, the one named last changes fastest.
Arguments:
- feats: bfloat16 [4096, 512], P('loop'), may hold values from -6 to 6
- tiles: bfloat16 [4, 8, 16, 128, 128], P('loop', 'wide'), may hold values from -0.1875 to 0.1875
- tile_rows: int32 [4, 8, 16], P('loop', 'wide'), may hold values from 0 to 7
- tile_cols: int32 [4, 8, 16], P('loop', 'wide'), may hold values from 0 to 3
- tile_count: int32 [4, 8], P('loop', 'wide'), may hold values from 1 to 16, as said below
- w_msg: bfloat16 [512, 512], replicated, may hold values from -0.25 to 0.25
- w_self: bfloat16 [512, 512], replicated, may hold values from -0.25 to 0.25
- readout: float32 [512], replicated, may hold values from -0.6 to 0.6
- labels: int32 [4096], P('loop'), may hold values from 0 to 1
Outputs:
- logits: float32 [4096], P('loop')
- grad_msg: bfloat16 [512, 512], replicated
- grad_self: bfloat16 [512, 512], replicated
Inputs may be any that keep to these rules, and one draw needn't show every extreme that they name: `tile_count`: some loop and wide index uses all 16 slots in every draw.
All inputs are finite; a program needn't handle non-finite values.
Results may differ from a plain program's by a relative error of at most 0.02.
Values may be sent and summed in bfloat16 or wider, within the bound.
A program may use at most 64 MiB of HBM per device.

v0:
```python
import functools

import jax
import jax.numpy as jnp
from jax import lax
from jax.experimental import pallas as pl
from jax.experimental.pallas import tpu as pltpu
from jax.sharding import PartitionSpec as P

CHUNKS = 4
G_CHUNKS = 2
ROW_STEP = 32


def kernel(
    nl, nw, ns, tb,
    feats, tiles, rows_in, cols_in, count_in, w_msg, w_self, readout_in, labels_in,
    out_logits, out_grads,
    t_rows, t_cols, t_count, readout, labels,
    gath, tiles_v, nf2, msg2, pg2, wm_v, ws_v, adj, part, sib_in, plane_out, plane_in, pre, trans,
    g_out, g_in, z_out, z_in, lg_buf,
    local_sem, send_sem, right_send, left_send, right_sem, left_sem, rs_sib_sem, rs_pl_sem, msg_sem, pg_sem, g_pl_sem, zr_sem, za_sem,
    ap_sem, as_sem, lg_sem,
):
    f32, bf16 = jnp.float32, jnp.bfloat16
    rows_dev, width = feats.shape
    nb = rows_dev // tb
    nch = nw // 2
    share = rows_dev // nw
    gshare = width // nch
    cw = width // CHUNKS
    gw = width // G_CHUNKS
    prow = z_in.shape[2]
    pieces = gshare // prow
    w = lax.axis_index("wide")
    l = lax.axis_index("loop")
    core = lax.rem(w, 2)
    chip = lax.div(w, 2)
    other = 1 - core
    sib = chip * 2 + other

    def cols(c):
        return pl.ds(c * cw, cw)

    def gcols(c):
        return pl.ds(c * gw, gw)

    def block_rows(q):
        return pl.ds(pl.multiple_of(q * tb, tb), tb)

    locs = [
        pltpu.make_async_copy(tiles, tiles_v, local_sem.at[0]),
        pltpu.make_async_copy(
            feats.at[pl.ds(pl.multiple_of(chip * 2 * share, 2 * share), 2 * share)], nf2,
            local_sem.at[1],
        ),
        pltpu.make_async_copy(w_self, ws_v, local_sem.at[2]),
        pltpu.make_async_copy(w_msg, wm_v, local_sem.at[3]),
        pltpu.make_async_copy(rows_in, t_rows, local_sem.at[4]),
        pltpu.make_async_copy(cols_in, t_cols, local_sem.at[5]),
        pltpu.make_async_copy(readout_in, readout, local_sem.at[6]),
        pltpu.make_async_copy(labels_in, labels, local_sem.at[7]),
        pltpu.make_async_copy(count_in, t_count, local_sem.at[8]),
    ]
    own_rows = pl.ds(pl.multiple_of(lax.rem(w, nb) * tb, tb), tb)
    own_copies = []
    for c in range(CHUNKS):
        own_copies.append(pltpu.make_async_copy(
            feats.at[own_rows, cols(c)],
            gath.at[c, block_rows(l)],
            local_sem.at[9 + c],
        ))
    for cp in locs + own_copies:
        cp.start()

    barrier = pltpu.get_barrier_semaphore()
    for d in range(1, nw):
        pl.semaphore_signal(barrier, inc=1, device_id={"wide": lax.rem(w + d, nw), "loop": l},
                            device_id_type=pl.DeviceIdType.MESH)
    for d in range(1, nl):
        pl.semaphore_signal(barrier, inc=1, device_id={"wide": w, "loop": lax.rem(l + d, nl)},
                            device_id_type=pl.DeviceIdType.MESH)
    pl.semaphore_wait(barrier, nw + nl - 2)

    sent = []

    def send(src, dst, recv, wide, loop):
        cp = pltpu.make_async_remote_copy(
            src_ref=src, dst_ref=dst, send_sem=send_sem.at[len(sent)], recv_sem=recv,
            device_id={"wide": wide, "loop": loop}, device_id_type=pl.DeviceIdType.MESH,
        )
        cp.start()
        sent.append(cp)
        return cp

    def chip_at(e):
        return lax.rem(chip + e + nch, nch)

    def loop_at(d):
        return lax.rem(l + d + nl, nl)

    maybe_sent = []

    def send_if(on, src, c, block, dist, to_right, step):
        send_s = (right_send if to_right else left_send).at[c, dist - 1]
        recv_s = (right_sem if to_right else left_sem).at[c, dist - 1]

        def make():
            return pltpu.make_async_remote_copy(
                src_ref=src(), dst_ref=gath.at[c, block_rows(block)], send_sem=send_s, recv_sem=recv_s,
                device_id={"wide": w, "loop": l + step if to_right else l - step},
                device_id_type=pl.DeviceIdType.MESH,
            )

        @pl.when(on)
        def _():
            make().start()

        maybe_sent.append((on, make))

    def wait_if(on, c, dist, from_left):
        @pl.when(on)
        def _():
            ref = gath.at[c, block_rows(l - dist if from_left else l + dist)]
            pltpu.make_async_remote_copy(
                src_ref=ref, dst_ref=ref, send_sem=send_sem.at[0],
                recv_sem=(right_sem if from_left else left_sem).at[c, dist - 1],
                device_id={"wide": w, "loop": l - 1 if from_left else l + 1},
                device_id_type=pl.DeviceIdType.MESH,
            ).wait_recv()

    relayed = range(2, nl - 1)
    for c in range(CHUNKS):
        for d in (2, 1):
            if d < nl:
                own = functools.partial(lambda c: feats.at[own_rows, cols(c)], c)
                send_if(l + d < nl, own, c, l, d, True, d)
                send_if(l >= d, own, c, l, d, False, d)

    def relay(c):
        for t in relayed:
            wait_if(l >= t, c, t, True)
            send_if(jnp.logical_and(l >= t, l + 1 < nl),
                    functools.partial(lambda c, t: gath.at[c, block_rows(l - t)], c, t),
                    c, l - t, t + 1, True, 1)
            wait_if(l + t < nl, c, t, False)
            send_if(jnp.logical_and(l + t < nl, l >= 1),
                    functools.partial(lambda c, t: gath.at[c, block_rows(l + t)], c, t),
                    c, l + t, t + 1, False, 1)

    def gathered(c):
        own_copies[c].wait()
        for t in range(1, nl):
            if t not in relayed:
                wait_if(l >= t, c, t, True)
                wait_if(l + t < nl, c, t, False)

    for k in (0, 4, 5, 8):
        locs[k].wait()
    cell = [
        jnp.where(s < t_count[0], t_rows[s] * nl + t_cols[s], -1) for s in range(ns)
    ]
    group = 4
    steps = tb // ROW_STEP

    def densify(i, carry):
        r = lax.div(i, steps)
        h = lax.rem(i, steps)
        first = r * tb + h * ROW_STEP
        share_id = lax.div(first, share)
        at = lax.div(share_id, 2) * share + lax.rem(first, share)
        for q0 in range(0, nl, group):
            accs = [jnp.zeros((ROW_STEP, tb), f32) for _ in range(group)]
            for s in range(ns):
                t = tiles_v[s, pl.ds(pl.multiple_of(h * ROW_STEP, ROW_STEP), ROW_STEP), :].astype(f32)
                for g in range(group):
                    on = jnp.where(cell[s] == r * nl + q0 + g, 1.0, 0.0).astype(f32)
                    accs[g] = accs[g] + on * t
            for g in range(group):
                adj[lax.rem(share_id, 2), pl.ds(pl.multiple_of(at, ROW_STEP), ROW_STEP),
                    pl.ds((q0 + g) * tb, tb)] = accs[g].astype(bf16)
        return carry

    lax.fori_loop(0, nb * steps // 2, densify, 0)
    relay(0)
    lax.fori_loop(nb * steps // 2, nb * steps, densify, 0)
    relay(1)

    sib_cp, pl_cp = [], []

    def partial_of(c):
        gathered(c)
        part[c, other] = jnp.dot(adj[other], gath[c], preferred_element_type=f32).astype(bf16)
        sib_cp.append(send(part.at[c, other], sib_in.at[c], rs_sib_sem.at[c], sib, l))
        part[c, core] = jnp.dot(adj[core], gath[c], preferred_element_type=f32).astype(bf16)

    def pair_sum(c, mine, theirs, out):
        out[c] = (mine[c, core].astype(f32) + theirs[c].astype(f32)).astype(bf16)

    def spread(c, out, land, sems, size):
        return [
            send(out.at[c, pl.ds(pl.multiple_of(chip_at(e) * size, size), size)],
                 land.at[c, e - 1], sems.at[c, e - 1], chip_at(e) * 2 + core, l)
            for e in range(1, nch)
        ]

    def total(c, out, land, size):
        acc = out[c, pl.ds(pl.multiple_of(chip * size, size), size), :].astype(f32)
        for e in range(1, nch):
            acc = acc + land[c, e - 1].astype(f32)
        return acc

    def to_chips(c):
        sib_cp[c].wait_recv()
        pair_sum(c, part, sib_in, plane_out)
        pl_cp.append(spread(c, plane_out, plane_in, rs_pl_sem, share))

    partial_of(0)
    for c in range(2, CHUNKS):
        relay(c)
        partial_of(c - 1)
        to_chips(c - 2)
    partial_of(CHUNKS - 1)
    to_chips(CHUNKS - 2)
    to_chips(CHUNKS - 1)

    for k in (1, 2, 3, 6, 7):
        locs[k].wait()
    mine = pl.ds(pl.multiple_of(core * share, share), share)
    nf = nf2[mine, :]
    pre[...] = jnp.dot(nf, ws_v[...], preferred_element_type=f32)

    @pl.when(core == 1)
    def _():
        trans[...] = nf2[...].astype(f32).T.astype(bf16)

    label_col = jnp.broadcast_to(
        labels[pl.ds(w, 1), :].astype(f32), (128, share)).T[:, :1]

    msg_cp = []
    for c in range(CHUNKS):
        for cp in pl_cp[c]:
            cp.wait_recv()
        msg = total(c, plane_out, plane_in, share).astype(bf16)
        pre[...] += jnp.dot(msg, wm_v[pl.ds(c * cw, cw), :], preferred_element_type=f32)
        msg2[mine, cols(c)] = msg
        ref = msg2.at[mine, cols(c)]
        msg_cp.append(send(ref, ref, msg_sem.at[c], sib, l))

    act = pre[...]
    gate = jax.nn.sigmoid(act)
    ro = readout[...]
    hidden = nf.astype(f32) + act * gate
    logit = jnp.sum(hidden * ro, axis=1, keepdims=True)
    resid = jax.nn.sigmoid(logit) - label_col
    pg = (resid * ro * gate * (1.0 + act * (1.0 - gate))).astype(bf16)

    pg_cp = []
    for c in range(G_CHUNKS):
        pg2[c, mine, :] = pg[:, c * gw:(c + 1) * gw]
        ref = pg2.at[c, mine]
        pg_cp.append(send(ref, ref, pg_sem.at[c], sib, l))
    for cp in msg_cp:
        cp.wait_recv()

    @pl.when(core == 0)
    def _():
        trans[...] = msg2[...].astype(f32).T.astype(bf16)

    pl_cp = []
    for c in range(G_CHUNKS):
        pg_cp[c].wait_recv()
        g_out[c] = jnp.dot(trans[...], pg2[c], preferred_element_type=f32).astype(bf16)
        pl_cp.append(spread(c, g_out, g_in, g_pl_sem, gshare))
    lg_buf[w] = jnp.broadcast_to(logit, (share, 128)).T[:8, :]
    lg_cp = [send(lg_buf.at[w], lg_buf.at[w], lg_sem.at[d - 1], lax.rem(w + d, nw), l)
             for d in range(1, nw)]

    zr_cp = []
    for c in range(G_CHUNKS):
        for cp in pl_cp[c]:
            cp.wait_recv()
        z_out[c] = total(c, g_out, g_in, gshare).astype(bf16)
        cps = []
        for d in range(1, nl):
            src = z_out.at[c]
            if pieces > 1:
                src = z_out.at[c, pl.ds(pl.multiple_of(loop_at(d) * prow, prow), prow)]
            cps.append(send(src, z_in.at[c, l], zr_sem.at[c, d - 1], w, loop_at(d)))
        zr_cp.append(cps)
        if pieces > 1:
            z_in[c, l] = z_out[c, pl.ds(pl.multiple_of(l * prow, prow), prow), :]
        else:
            z_in[c, l] = z_out[c]

    def piece(which, d):
        at = loop_at(-d) * prow if pieces > 1 else 0
        return core * nch + which, pl.ds(pl.multiple_of(at, prow), prow)

    za_cp, ap_cp, as_cp = [], [], []

    def to_plane(c, d):
        who, rws = piece(chip, d)
        ref = out_grads.at[who, rws, gcols(c)]
        cps = [send(ref, ref, ap_sem.at[c, d, e - 1], chip_at(e) * 2 + core, l)
               for e in range(1, nch)]
        as_cp.append(send(ref, ref, as_sem.at[c, d, 0], sib, l))
        return cps

    for c in range(G_CHUNKS):
        for cp in zr_cp[c]:
            cp.wait_recv()
        acc = z_in[c, 0].astype(f32)
        for k in range(1, nl):
            acc = acc + z_in[c, k].astype(f32)
        who, rws = piece(chip, 0)
        out_grads[who, rws, gcols(c)] = acc.astype(bf16)
        ref = out_grads.at[who, rws, gcols(c)]
        if pieces > 1:
            za_cp.append([send(ref, ref, za_sem.at[c, d - 1], w, loop_at(d))
                          for d in range(1, nl)])
        ap_cp.append([to_plane(c, 0)])
    for d in range(1, pieces):
        for c in range(G_CHUNKS):
            za_cp[c][d - 1].wait_recv()
            ap_cp[c].append(to_plane(c, d))
    for d in range(pieces):
        for c in range(G_CHUNKS):
            for e in range(1, nch):
                ap_cp[c][d][e - 1].wait_recv()
                who, rws = piece(chip_at(-e), d)
                ref = out_grads.at[who, rws, gcols(c)]
                as_cp.append(send(ref, ref, as_sem.at[c, d, e], sib, l))

    for cp in lg_cp:
        cp.wait_recv()
    for k in range(nw):
        out_logits[pl.ds(k, 1), :] = lg_buf[k, :1, :]
    for cp in as_cp:
        cp.wait_recv()
    for cp in sent:
        cp.wait_send()
    for on, make in maybe_sent:
        pl.when(on)(functools.partial(lambda make: make().wait_send(), make))


def body(feats, tiles, tile_rows, tile_cols, tile_count, w_msg, w_self, readout, labels):
    rows_dev, width = feats.shape
    tb = tiles.shape[-1]
    ns = tiles.shape[2]
    nw, nl = lax.axis_size("wide"), lax.axis_size("loop")
    nch = nw // 2
    share = rows_dev // nw
    gshare = width // nch
    cw = width // CHUNKS
    gw = width // G_CHUNKS
    prow = gshare // nl
    if prow < 16:
        prow = gshare
    pieces = gshare // prow
    bf16, f32 = jnp.bfloat16, jnp.float32
    sends = (
        CHUNKS * (nch + 1) + G_CHUNKS * nch + nw - 1 + 2 * G_CHUNKS * (nl - 1)
        + G_CHUNKS * pieces * (2 * nch - 1)
    )
    vmem = pl.BlockSpec(memory_space=pltpu.VMEM)
    hbm = pl.BlockSpec(memory_space=pltpu.HBM)
    dma = pltpu.SemaphoreType.DMA
    logits, grads = pl.pallas_call(
        functools.partial(kernel, nl, nw, ns, tb),
        out_shape=(
            jax.ShapeDtypeStruct((nw, share), f32),
            jax.ShapeDtypeStruct((nw, gshare, width), bf16),
        ),
        in_specs=[hbm] * 9,
        out_specs=(vmem, vmem),
        scratch_shapes=[
            pltpu.SMEM((ns,), jnp.int32),
            pltpu.SMEM((ns,), jnp.int32),
            pltpu.SMEM((1,), jnp.int32),
            pltpu.VMEM((1, width), f32),
            pltpu.VMEM((nw, share), jnp.int32),
            pltpu.VMEM((CHUNKS, nl * tb, cw), bf16),
            pltpu.VMEM((ns, tb, tb), bf16),
            pltpu.VMEM((2 * share, width), bf16),
            pltpu.VMEM((2 * share, width), bf16),
            pltpu.VMEM((G_CHUNKS, 2 * share, gw), bf16),
            pltpu.VMEM((width, width), bf16),
            pltpu.VMEM((width, width), bf16),
            pltpu.VMEM((2, nch * share, nl * tb), bf16),
            pltpu.VMEM((CHUNKS, 2, nch * share, cw), bf16),
            pltpu.VMEM((CHUNKS, nch * share, cw), bf16),
            pltpu.VMEM((CHUNKS, nch * share, cw), bf16),
            pltpu.VMEM((CHUNKS, nch - 1, share, cw), bf16),
            pltpu.VMEM((share, width), f32),
            pltpu.VMEM((width, 2 * share), bf16),
            pltpu.VMEM((G_CHUNKS, nch * gshare, gw), bf16),
            pltpu.VMEM((G_CHUNKS, nch - 1, gshare, gw), bf16),
            pltpu.VMEM((G_CHUNKS, gshare, gw), bf16),
            pltpu.VMEM((G_CHUNKS, nl, prow, gw), bf16),
            pltpu.VMEM((nw, 8, share), f32),
            dma((9 + CHUNKS,)),
            dma((sends,)),
            dma((CHUNKS, nl - 1)),
            dma((CHUNKS, nl - 1)),
            dma((CHUNKS, nl - 1)),
            dma((CHUNKS, nl - 1)),
            dma((CHUNKS,)),
            dma((CHUNKS, nch - 1)),
            dma((CHUNKS,)),
            dma((G_CHUNKS,)),
            dma((G_CHUNKS, nch - 1)),
            dma((G_CHUNKS, nl - 1)),
            dma((G_CHUNKS, nl - 1)),
            dma((G_CHUNKS, pieces, nch - 1)),
            dma((G_CHUNKS, pieces, nch)),
            dma((nw - 1,)),
        ],
        compiler_params=pltpu.CompilerParams(
            collective_id=0, has_side_effects=True
        ),
    )(
        feats, tiles.reshape(ns, tb, tb), tile_rows.reshape(ns), tile_cols.reshape(ns),
        tile_count.reshape(1), w_msg, w_self, readout.reshape(1, width),
        labels.reshape(nw, share),
    )
    both = grads.reshape(2, width, width)
    return logits.reshape(rows_dev), both[0], both[1]


def solution(mesh):
    placed = (
        P("loop", None),
        P("loop", "wide", None, None, None),
        P("loop", "wide", None),
        P("loop", "wide", None),
        P("loop", "wide"),
        P(),
        P(),
        P(),
        P("loop"),
    )
    return jax.shard_map(
        body, mesh=mesh, in_specs=placed, out_specs=(P("loop"), P(), P()), check_vma=False
    )
```

profile of v0, /device:TPU:1, one launch (start us, length us, event | category | flops | bytes accessed | tf_op | source)
XLA Modules:
  0.0 54.1 jit_solution(13366152472994756956)
XLA Ops:
  1.3 49.4 %shard_map.112 = (f32[8,128]{1,0:T(8,128)}, bf16[8,128,512]{2,1,0:T(8,128)(2,1)}) custom-call(bf16[1024,512]{1,0:T(8,128)(2,1)} %feats.1, bf16[16,128,128]{2,1,0:T(8,128)(2,1)} %bitcast.10, s32[16]{0:T(128)} %bitcast.16, s32[16]{0:T(128)} %bitcast.17, s32[1]{0:T(128)} %bitcast.9.count_in, bf16[512,512]{1,0:T(8,128)(2,1)} %w_msg.1, bf16[512,512]{1,0:T(8,128)(2,1)} %w_self.1, ...), custom_call_target="tpu_custom_call" | custom-call | tf_op jit(solution)/shard_map/pallas_call | solution.py:369
  50.6 2.2 %fusion = (bf16[4,128,512]{2,1,0:T(8,128)(2,1)}, bf16[4,128,512]{2,1,0:T(8,128)(2,1)}) fusion(bf16[8,128,512]{2,1,0:T(8,128)(2,1)} %get-tuple-element.6), kind=kLoop, calls=%fused_computation | loop fusion | bytes 2097152 | tf_op jit(solution)/shard_map/slice | solution.py:428
  52.9 0.0 copy-start
  52.9 0.7 %copy-done = f32[8,128]{1,0:T(8,128)S(1)} copy-done((f32[8,128]{1,0:T(8,128)S(1)}, f32[8,128]{1,0:T(8,128)}, u32[]{:S(2)}) %copy-start) | copy-done | bytes 4120
  53.6 0.6 %copy.14 = f32[1024]{0:T(1024)} copy(f32[1024]{0:T(1024)S(1)} %bitcast.14) | data formatting | bytes 8192
Async XLA Ops:
  52.9 0.7 %copy-start = (f32[8,128]{1,0:T(8,128)S(1)}, f32[8,128]{1,0:T(8,128)}, u32[]{:S(2)}) copy-start(f32[8,128]{1,0:T(8,128)} %get-tuple-element.5) | copy-start | bytes 12292
where the time goes:
time: 54.3 us; the launch traced here: 54.1 us
  Pallas kernels  49.4 us (91%)
  local copies, waits for them, and re-layouts  3.51 us (6%)
  between operations  1.29 us (2%)
    pallas_call x1, Pallas kernels, body(): pl.pallas_call(functools.partial(kernel, nl, nw, ns, tb), out_shape=(jax....  49.4 us
    slice x1, local copies, waits for them, and re-layouts, body(): return (logits.reshape(rows_dev), both[0], both[1])  2.23 us
    unnamed x3, local copies, waits for them, and re-layouts  1.27 us

commit v1 on v0

--- a/solution.py
+++ b/solution.py
@@ -8,7 +8,7 @@
 from jax.sharding import PartitionSpec as P
 
 CHUNKS = 4
-G_CHUNKS = 2
+G_CHUNKS = 4
 ROW_STEP = 32
 
 
@@ -276,8 +276,9 @@
     lg_cp = [send(lg_buf.at[w], lg_buf.at[w], lg_sem.at[d - 1], lax.rem(w + d, nw), l)
              for d in range(1, nw)]
 
-    zr_cp = []
-    for c in range(G_CHUNKS):
+    zr_cp, za_cp, ap_cp, as_cp = [], [], [], []
+
+    def loop_reduce(c):
         for cp in pl_cp[c]:
             cp.wait_recv()
         z_out[c] = total(c, g_out, g_in, gshare).astype(bf16)
@@ -293,44 +294,37 @@
         else:
             z_in[c, l] = z_out[c]
 
-    def piece(which, d):
-        at = loop_at(-d) * prow if pieces > 1 else 0
-        return core * nch + which, pl.ds(pl.multiple_of(at, prow), prow)
-
-    za_cp, ap_cp, as_cp = [], [], []
-
-    def to_plane(c, d):
-        who, rws = piece(chip, d)
-        ref = out_grads.at[who, rws, gcols(c)]
-        cps = [send(ref, ref, ap_sem.at[c, d, e - 1], chip_at(e) * 2 + core, l)
-               for e in range(1, nch)]
-        as_cp.append(send(ref, ref, as_sem.at[c, d, 0], sib, l))
-        return cps
-
-    for c in range(G_CHUNKS):
+    def loop_gather(c):
         for cp in zr_cp[c]:
             cp.wait_recv()
         acc = z_in[c, 0].astype(f32)
         for k in range(1, nl):
             acc = acc + z_in[c, k].astype(f32)
-        who, rws = piece(chip, 0)
-        out_grads[who, rws, gcols(c)] = acc.astype(bf16)
-        ref = out_grads.at[who, rws, gcols(c)]
-        if pieces > 1:
-            za_cp.append([send(ref, ref, za_sem.at[c, d - 1], w, loop_at(d))
-                          for d in range(1, nl)])
-        ap_cp.append([to_plane(c, 0)])
-    for d in range(1, pieces):
-        for c in range(G_CHUNKS):
-            za_cp[c][d - 1].wait_recv()
-            ap_cp[c].append(to_plane(c, d))
-    for d in range(pieces):
-        for c in range(G_CHUNKS):
-            for e in range(1, nch):
-                ap_cp[c][d][e - 1].wait_recv()
-                who, rws = piece(chip_at(-e), d)
-                ref = out_grads.at[who, rws, gcols(c)]
-                as_cp.append(send(ref, ref, as_sem.at[c, d, e], sib, l))
+        at = l * prow if pieces > 1 else 0
+        rws = pl.ds(pl.multiple_of(at, prow), prow)
+        out_grads[core * nch + chip, rws, gcols(c)] = acc.astype(bf16)
+        ref = out_grads.at[core * nch + chip, rws, gcols(c)]
+        za_cp.append([send(ref, ref, za_sem.at[c, d - 1], w, loop_at(d))
+                      for d in range(1, nl)] if pieces > 1 else [])
+
+    def chip_gather(c):
+        for cp in za_cp[c]:
+            cp.wait_recv()
+        ref = out_grads.at[core * nch + chip, :, gcols(c)]
+        ap_cp.append([send(ref, ref, ap_sem.at[c, e - 1], chip_at(e) * 2 + core, l)
+                      for e in range(1, nch)])
+        as_cp.append(send(ref, ref, as_sem.at[c, 0], sib, l))
+
+    def core_gather(c):
+        for e in range(1, nch):
+            ap_cp[c][e - 1].wait_recv()
+            ref = out_grads.at[core * nch + chip_at(-e), :, gcols(c)]
+            as_cp.append(send(ref, ref, as_sem.at[c, e], sib, l))
+
+    for i in range(G_CHUNKS + 4):
+        for stage, late in ((loop_reduce, 0), (loop_gather, 1), (chip_gather, 2), (core_gather, 4)):
+            if 0 <= i - late < G_CHUNKS:
+                stage(i - late)
 
     for cp in lg_cp:
         cp.wait_recv()
@@ -357,11 +351,10 @@
     prow = gshare // nl
     if prow < 16:
         prow = gshare
-    pieces = gshare // prow
     bf16, f32 = jnp.bfloat16, jnp.float32
     sends = (
         CHUNKS * (nch + 1) + G_CHUNKS * nch + nw - 1 + 2 * G_CHUNKS * (nl - 1)
-        + G_CHUNKS * pieces * (2 * nch - 1)
+        + G_CHUNKS * (2 * nch - 1)
     )
     vmem = pl.BlockSpec(memory_space=pltpu.VMEM)
     hbm = pl.BlockSpec(memory_space=pltpu.HBM)
@@ -369,8 +362,8 @@
     logits, grads = pl.pallas_call(
         functools.partial(kernel, nl, nw, ns, tb),
         out_shape=(
-            jax.ShapeDtypeStruct((nw, share), f32),
-            jax.ShapeDtypeStruct((nw, gshare, width), bf16),
+            pltpu.VMEM((nw, share), f32),
+            pltpu.VMEM((nw, gshare, width), bf16),
         ),
         in_specs=[hbm] * 9,
         out_specs=(vmem, vmem),
@@ -412,12 +405,12 @@
             dma((G_CHUNKS, nch - 1)),
             dma((G_CHUNKS, nl - 1)),
             dma((G_CHUNKS, nl - 1)),
-            dma((G_CHUNKS, pieces, nch - 1)),
-            dma((G_CHUNKS, pieces, nch)),
+            dma((G_CHUNKS, nch - 1)),
+            dma((G_CHUNKS, nch)),
             dma((nw - 1,)),
         ],
         compiler_params=pltpu.CompilerParams(
-            collective_id=0, has_side_effects=True
+            collective_id=0, has_side_effects=True, vmem_limit_bytes=60 * 2**20
         ),
     )(
         feats, tiles.reshape(ns, tb, tb), tile_rows.reshape(ns), tile_cols.reshape(ns),

time: 54.3 us -> 52.5 us (0.967)
  local copies, waits for them, and re-layouts: 3.51 us -> 1.63 us
    slice x1, local copies, waits for them, and re-layouts: 2.23 us -> 1.03 us  [body(): return (logits.reshape(rows_dev), both[0], both[1])]
    unnamed x3 -> x1, local copies, waits for them, and re-layouts: 1.27 us -> 0.6 us
where the time goes in v1:
time: 52.5 us; the launch traced here: 52.3 us
  Pallas kernels  49.4 us (94%)
  local copies, waits for them, and re-layouts  1.63 us (3%)
  between operations  1.29 us (2%)
    pallas_call x1, Pallas kernels, body(): pl.pallas_call(functools.partial(kernel, nl, nw, ns, tb), out_shape=(pltp...  49.4 us

profile of v1, /device:TPU:1, one launch (start us, length us, event | category | flops | bytes accessed | tf_op | source)
XLA Modules:
  0.0 52.3 jit_solution(9624123640270995712)
XLA Ops:
  1.3 49.4 %shard_map.112 = (f32[8,128]{1,0:T(8,128)S(1)}, bf16[8,128,512]{2,1,0:T(8,128)(2,1)S(1)}) custom-call(bf16[1024,512]{1,0:T(8,128)(2,1)} %feats.1, bf16[16,128,128]{2,1,0:T(8,128)(2,1)} %bitcast.11, s32[16]{0:T(128)} %bitcast.16, s32[16]{0:T(128)} %bitcast.17, s32[1]{0:T(128)} %bitcast.9.count_in, bf16[512,512]{1,0:T(8,128)(2,1)} %w_msg.1, ...), custom_call_target="tpu_custom_call" | custom-call | tf_op jit(solution)/shard_map/pallas_call | solution.py:362
  50.7 0.6 %copy.13 = f32[1024]{0:T(1024)} copy(f32[1024]{0:T(1024)S(1)} %bitcast.10) | data formatting | bytes 8192
  51.3 1.0 %fusion = (bf16[4,128,512]{2,1,0:T(8,128)(2,1)}, bf16[4,128,512]{2,1,0:T(8,128)(2,1)}) fusion(bf16[8,128,512]{2,1,0:T(8,128)(2,1)S(1)} %get-tuple-element.6), kind=kLoop, calls=%fused_computation | loop fusion | bytes 2097152 | tf_op jit(solution)/shard_map/slice | solution.py:421
